TPU v7x, 32 devices: a whole 2x2x4 slice. The times are simulated.
32 devices in a mesh: py: 8 (over z, x), pz: 4 (over y, core).
Axes of the slice: x: 2, y: 2, z: 4, core: 2. Of those that a mesh axis runs over, the one named last changes fastest.
Arguments:
- velocity: float32 [3, 288, 160, 2048], P(None, 'pz', 'py'), may hold values from -40 to 40
Outputs:
- filtered_velocity: float32 [3, 32, 16, 256], P(None, None, 'pz', 'py')
- stresses: float32 [6, 32, 16, 256], P(None, None, 'pz', 'py')
All inputs are finite; a program needn't handle non-finite values.
Results may differ from a plain program's by a relative error of at most 0.00007.
Values sent between devices are 32-bit elements; how exact they have to be, the bound alone decides.
A program may use at most 192 MiB of HBM per device.

v0:
```python
import jax
import jax.numpy as jnp
from jax import lax
from jax.sharding import PartitionSpec as P

spread_cells = 8.0
stress_pairs = ((0, 0), (0, 1), (0, 2), (1, 1), (1, 2), (2, 2))
highest = lax.Precision.HIGHEST


def gauss_norm():
    tap_range = jnp.arange(-16, 17).astype(jnp.float32)
    return jnp.sum(jnp.exp(-tap_range * tap_range / (2.0 * spread_cells * spread_cells)))


def taps_matrix(n_outputs):
    n_inputs = 8 * n_outputs + 32
    offsets = (
        jnp.arange(n_inputs).astype(jnp.float32)[:, None]
        - 8.0 * jnp.arange(n_outputs).astype(jnp.float32)[None, :]
        - 16.0
    )
    weights = jnp.exp(-offsets * offsets / (2.0 * spread_cells * spread_cells)) / gauss_norm()
    return jnp.where(jnp.abs(offsets) <= 16.0, weights, 0.0)


def circulant_taps(n_cells):
    n_outputs = n_cells // 8
    cell_idx = jnp.arange(n_cells)[:, None]
    out_idx = jnp.arange(n_outputs)[None, :]
    wrapped = jnp.remainder(cell_idx - 8 * out_idx + n_cells // 2, n_cells) - n_cells // 2
    offsets = wrapped.astype(jnp.float32)
    weights = jnp.exp(-offsets * offsets / (2.0 * spread_cells * spread_cells)) / gauss_norm()
    return jnp.where(jnp.abs(offsets) <= 16.0, weights, 0.0)


def filter_first(fields):
    n_fields, plane_rows, line_rows, n_cells = fields.shape
    result = jnp.einsum("fzyn,nk->kyfz", fields, circulant_taps(n_cells), precision=highest)
    return result.reshape(n_cells // 8, line_rows, n_fields * plane_rows)


def filter_second(moved):
    y_total = moved.shape[1]
    return jnp.einsum("kym,yj->kjm", moved, taps_matrix((y_total - 32) // 8), precision=highest)


def split_fields(both, n_fields_a, plane_rows):
    grouped = both.reshape(both.shape[0], both.shape[1], 9, plane_rows)
    first_part = grouped[:, :, 0:n_fields_a].reshape(both.shape[0], both.shape[1], -1)
    second_part = grouped[:, :, n_fields_a:9].reshape(both.shape[0], both.shape[1], -1)
    return (first_part, second_part)


def filter_third(moved, n_fields, n_sources, plane_rows):
    z_total = n_sources * plane_rows
    grouped = moved.reshape(moved.shape[0], moved.shape[1], n_sources, n_fields, plane_rows)
    table = taps_matrix((z_total - 32) // 8).reshape(n_sources, plane_rows, -1)
    return jnp.einsum("kjsfz,szi->fijk", grouped, table, precision=highest)


def on_device(velocity):
    plane_rows = velocity.shape[1]
    products = jnp.stack(
        [velocity[first_comp] * velocity[second_comp] for first_comp, second_comp in stress_pairs]
    )
    vel_first = filter_first(velocity)
    prod_first = filter_first(products)
    merged = jnp.concatenate([vel_first, prod_first], axis=2)
    moved = lax.all_to_all(merged, "py", split_axis=0, concat_axis=1, tiled=True)
    both_second = filter_second(moved)
    vel_second, prod_second = split_fields(both_second, 3, plane_rows)
    n_sources = lax.axis_size("pz")
    vel_planes, prod_planes = (
        lax.all_to_all(vel_second, "pz", split_axis=1, concat_axis=2, tiled=True),
        lax.all_to_all(prod_second, "pz", split_axis=1, concat_axis=2, tiled=True),
    )
    filtered_velocity = filter_third(vel_planes, 3, n_sources, plane_rows)
    filtered_products = filter_third(prod_planes, 6, n_sources, plane_rows)
    stresses = jnp.stack(
        [
            filtered_products[pair_index]
            - filtered_velocity[first_comp] * filtered_velocity[second_comp]
            for pair_index, (first_comp, second_comp) in enumerate(stress_pairs)
        ]
    )
    return (filtered_velocity, stresses)


def solution(mesh):
    placed = (P(None, "pz", "py", None),)
    return jax.shard_map(
        on_device,
        mesh=mesh,
        in_specs=placed,
        out_specs=(P(None, None, "pz", "py"), P(None, None, "pz", "py")),
        check_vma=False,
    )
```

profile of v0, /device:TPU:0, one launch (start us, length us, event | category | flops | bytes accessed | tf_op | source)
XLA Modules:
  0.0 703.8 jit_solution(7904877954452540442)
XLA Ops:
  0.6 0.6 fusion.85
  1.2 11.3 %multiply_dynamic-update-slice_fusion.5 = f32[6,72,20,2048]{3,1,2,0:T(8,128)} fusion(f32[3,72,20,2048]{3,1,2,0:T(8,128)} %param.1), kind=kLoop, calls=%fused_computation.8 | loop fusion | flops 2949119 | bytes 23592960
  12.5 13.6 %multiply_dynamic-update-slice_fusion.4 = f32[6,72,20,2048]{3,1,2,0:T(8,128)} fusion(f32[6,72,20,2048]{3,1,2,0:T(8,128)} %multiply_dynamic-update-slice_fusion.5, f32[3,72,20,2048]{3,1,2,0:T(8,128)} %param.1), kind=kLoop, calls=%fused_computation.7 | loop fusion | flops 2949120 | bytes 35389440
  26.1 13.6 %multiply_dynamic-update-slice_fusion.3 = f32[6,72,20,2048]{3,1,2,0:T(8,128)} fusion(f32[6,72,20,2048]{3,1,2,0:T(8,128)} %multiply_dynamic-update-slice_fusion.4, f32[3,72,20,2048]{3,1,2,0:T(8,128)} %param.1), kind=kLoop, calls=%fused_computation.6 | loop fusion | flops 2949120 | bytes 35389440
  39.8 11.2 %multiply_dynamic-update-slice_fusion.2 = f32[6,72,20,2048]{3,1,2,0:T(8,128)} fusion(f32[6,72,20,2048]{3,1,2,0:T(8,128)} %multiply_dynamic-update-slice_fusion.3, f32[3,72,20,2048]{3,1,2,0:T(8,128)} %param.1), kind=kLoop, calls=%fused_computation.5 | loop fusion | flops 2949120 | bytes 23592960
  50.9 13.6 %multiply_dynamic-update-slice_fusion.1 = f32[6,72,20,2048]{3,1,2,0:T(8,128)} fusion(f32[6,72,20,2048]{3,1,2,0:T(8,128)} %multiply_dynamic-update-slice_fusion.2, f32[3,72,20,2048]{3,1,2,0:T(8,128)} %param.1), kind=kLoop, calls=%fused_computation.4 | loop fusion | flops 2949120 | bytes 35389440
  64.5 11.1 %multiply_dynamic-update-slice_fusion = f32[6,72,20,2048]{3,1,2,0:T(8,128)} fusion(f32[6,72,20,2048]{3,1,2,0:T(8,128)} %multiply_dynamic-update-slice_fusion.1, f32[3,72,20,2048]{3,1,2,0:T(8,128)} %param.1), kind=kLoop, calls=%fused_computation.3 | loop fusion | flops 2949120 | bytes 23592960 | tf_op jit(solution)/shard_map/stack | solution.py:64
  75.6 36.9 %convolution_bitcast_fusion.1 = f32[256,20,3,72]{0,3,1,2:T(8,128)S(1)} fusion(f32[3,72,20,2048]{3,1,2,0:T(8,128)} %param.1, f32[]{:T(128)} %fusion.85, s32[256]{0:T(256)S(1)} %iota_multiply_fusion), kind=kOutput, calls=%fused_computation.14 | convolution fusion | flops 27190624256 | bytes 39814148 | tf_op jit(solution)/shard_map/fzyn,nk->kyfz/dot_general | solution.py:39
  112.6 67.5 %convolution_bitcast_fusion = f32[256,20,6,72]{0,3,1,2:T(8,128)S(1)} fusion(f32[6,72,20,2048]{3,1,2,0:T(8,128)} %multiply_dynamic-update-slice_fusion, f32[]{:T(128)} %fusion.85, s32[256]{0:T(256)S(1)} %iota_multiply_fusion), kind=kOutput, calls=%fused_computation.9 | convolution fusion | flops 54369714176 | bytes 79627264 | tf_op jit(solution)/shard_map/fzyn,nk->kyfz/dot_general | solution.py:39
  180.1 4.3 copy.17
  184.4 2.4 copy.16
  186.8 10.5 %pad_maximum_fusion = f32[256,20,648]{0,2,1:T(8,128)} fusion(f32[256,20,432]{0,2,1:T(8,128)} %bitcast.60, f32[256,20,216]{0,2,1:T(8,128)} %bitcast.61), kind=kLoop, calls=%fused_computation.2 | loop fusion | flops 3317760 | bytes 26542080 | tf_op jit(solution)/shard_map/concatenate | solution.py:69
  197.3 18.0 %copy.18 = f32[256,20,648]{2,1,0:T(8,128)} copy(f32[256,20,648]{0,2,1:T(8,128)} %pad_maximum_fusion) | data formatting | bytes 26542080 | tf_op jit(solution)/shard_map/concatenate | solution.py:69
  215.4 7.3 %all-to-all-start = ((f32[256,20,648]{2,1,0:T(8,128)}), f32[256,20,648]{2,1,0:T(8,128)}, u32[]{:S(2)}, u32[]{:S(2)}) async-start(f32[256,20,648]{2,1,0:T(8,128)} %copy.18), calls=%async_computation | async-start | bytes 37748736 | tf_op jit(solution)/shard_map/all_to_all | solution.py:70
  222.6 408.5 %all-to-all-done = f32[256,20,648]{2,1,0:T(8,128)} async-done(((f32[256,20,648]{2,1,0:T(8,128)}), f32[256,20,648]{2,1,0:T(8,128)}, u32[]{:S(2)}, u32[]{:S(2)}) %all-to-all-start) | async-done | bytes 13271072 | tf_op jit(solution)/shard_map/all_to_all | solution.py:70
  631.2 11.3 %copy.20 = f32[32,8,20,648]{3,0,2,1:T(8,128)S(1)} copy(f32[32,8,20,648]{3,2,0,1:T(8,128)} %bitcast.12) | data formatting | bytes 26542080 | tf_op jit(solution)/shard_map/all_to_all | solution.py:70
  642.4 16.9 %fusion.14 = f32[32,16,648]{2,1,0:T(8,128)S(1)} fusion(f32[32,160,648]{2,0,1:T(8,128)S(1)} %bitcast.59, f32[]{:T(128)} %fusion.85, f32[16]{0:T(128)S(1)} %convert_multiply_fusion, f32[160]{0:T(256)S(1)} %iota_convert_fusion), kind=kOutput, calls=%fused_computation.26 | convolution fusion | flops 637032960 | bytes 14598852 | tf_op jit(solution)/shard_map/kym,yj->kjm/dot_general | solution.py:45
  659.3 3.4 reshape.79
  662.7 1.8 slice.74
  664.8 1.1 copy.22
  665.9 4.1 all-to-all-start.1
  670.1 2.5 slice.75
  673.0 1.6 copy.25
  674.6 4.4 all-to-all-done.1
  679.0 3.7 all-to-all-start.2
  682.8 1.1 copy.48
  684.3 2.6 convolution_bitcast_fusion.2
  686.9 0.8 copy.28
  687.7 9.4 %all-to-all-done.2 = f32[32,16,432]{2,0,1:T(8,128)S(1)} async-done(((f32[32,16,432]{2,0,1:T(8,128)}), f32[32,16,432]{2,0,1:T(8,128)S(1)}, u32[]{:S(2)}, u32[]{:S(2)}) %all-to-all-start.2) | async-done | bytes 884768 | tf_op jit(solution)/shard_map/all_to_all | solution.py:76
  697.2 0.7 reshape.83
  697.9 4.5 fusion.17
  702.5 1.0 copy.29
  (15 shorter events, 1.5 us)
Async XLA Ops:
  215.4 415.8 %all-to-all-start = ((f32[256,20,648]{2,1,0:T(8,128)}), f32[256,20,648]{2,1,0:T(8,128)}, u32[]{:S(2)}, u32[]{:S(2)}) async-start(f32[256,20,648]{2,1,0:T(8,128)} %copy.18), calls=%async_computation | async-start | bytes 37748736 | tf_op jit(solution)/shard_map/all_to_all | solution.py:70
  665.9 13.1 %all-to-all-start.1 = ((f32[32,16,216]{2,0,1:T(8,128)}), f32[32,16,216]{2,0,1:T(8,128)}, u32[]{:S(2)}, u32[]{:S(2)}) async-start(f32[32,16,216]{2,0,1:T(8,128)} %copy.22), calls=%async_computation.1 | async-start | bytes 1048576 | tf_op jit(solution)/shard_map/all_to_all | solution.py:75
  679.0 18.1 %all-to-all-start.2 = ((f32[32,16,432]{2,0,1:T(8,128)}), f32[32,16,432]{2,0,1:T(8,128)S(1)}, u32[]{:S(2)}, u32[]{:S(2)}) async-start(f32[32,16,432]{2,0,1:T(8,128)} %copy.25), calls=%async_computation.2 | async-start | bytes 2097152 | tf_op jit(solution)/shard_map/all_to_all | solution.py:76
where the time goes:
time: 710 us; the launch traced here: 704 us
  waiting for transfers between devices  422 us (59%)
  matrix products  128 us (18%)
  other arithmetic  85.6 us (12%)
  local copies, waits for them, and re-layouts  51.3 us (7%)
  starting transfers between devices  15.1 us (2%)
    all_to_all x1, waiting for transfers between devices, on_device(): lax.all_to_all(merged, 'py', split_axis=0, concat_axis=1, tiled=True)  409 us
    dot_general x2, matrix products, filter_first(): jnp.einsum('fzyn,nk->kyfz', fields, circulant_taps(n_cells), precision=hi...  104 us
    unnamed x10, other arithmetic  63.3 us
    concatenate x1, local copies, waits for them, and re-layouts, on_device(): merged = jnp.concatenate([vel_first, prod_first], axis=2)  18 us
    dot_general x1, matrix products, filter_second(): jnp.einsum('kym,yj->kjm', moved, taps_matrix((y_total - 32) // 8), precis...  16.9 us
  transfers between devices with their start and end apart: 3, of which 3 were waited for; matrix products, arithmetic and copies ran while one was open for 1% of the time, Pallas kernels for 0%

commit v1 on v0

--- a/solution.py
+++ b/solution.py
@@ -6,6 +6,28 @@
 spread_cells = 8.0
 stress_pairs = ((0, 0), (0, 1), (0, 2), (1, 1), (1, 2), (2, 2))
 highest = lax.Precision.HIGHEST
+
+
+def in_blocks(array, dim, size):
+    before, after = (array.shape[:dim], array.shape[dim + 1 :])
+    return jnp.moveaxis(array.reshape(*before, size, -1, *after), dim, 0)
+
+
+def laid_out(pieces, dim):
+    pieces = jnp.moveaxis(pieces, 0, dim)
+    lengths = pieces.shape
+    return pieces.reshape(*lengths[:dim], lengths[dim] * lengths[dim + 1], *lengths[dim + 2 :])
+
+
+def exchange_in_pairs(shard, axis, split_dim, concat_dim):
+    size, mine = (lax.axis_size(axis), lax.axis_index(axis))
+    tiles = in_blocks(shard, split_dim, size)
+    finished = [tiles[mine]]
+    for hop in range(1, size):
+        sent = tiles[mine ^ hop]
+        finished.append(lax.ppermute(sent, axis, [(i, i ^ hop) for i in range(size)]))
+    tiles = jnp.stack(finished)[mine ^ jnp.arange(size)]
+    return laid_out(tiles, concat_dim)
 
 
 def gauss_norm():
@@ -67,7 +89,7 @@
     vel_first = filter_first(velocity)
     prod_first = filter_first(products)
     merged = jnp.concatenate([vel_first, prod_first], axis=2)
-    moved = lax.all_to_all(merged, "py", split_axis=0, concat_axis=1, tiled=True)
+    moved = exchange_in_pairs(merged, "py", 0, 1)
     both_second = filter_second(moved)
     vel_second, prod_second = split_fields(both_second, 3, plane_rows)
     n_sources = lax.axis_size("pz")

time: 710 us -> 677 us (0.954)
  the two profiles are of different devices: /device:TPU:0 before, /device:TPU:16 now
where the time goes in v1:
time: 677 us; the launch traced here: 670 us
  waiting for transfers between devices  328 us (48%)
  matrix products  135 us (20%)
  local copies, waits for them, and re-layouts  101 us (15%)
  other arithmetic  88.7 us (13%)
  starting transfers between devices  15.7 us (2%)
    ppermute x7, waiting for transfers between devices, exchange_in_pairs(): lax.ppermute(sent, axis, [(i, i ^ hop) for i in range(size)])  315 us
    dot_general x2, matrix products, filter_first(): jnp.einsum('fzyn,nk->kyfz', fields, circulant_taps(n_cells), precision=hi...  106 us
    unnamed x11, other arithmetic  66.8 us
    concatenate x2, local copies, waits for them, and re-layouts, on_device(): merged = jnp.concatenate([vel_first, prod_first], axis=2)  30 us
    transpose x2, local copies, waits for them, and re-layouts, filter_first(): jnp.einsum('fzyn,nk->kyfz', fields, circulant_taps(n_cells), precision=hi...  24.5 us
    dot_general x1, matrix products, filter_second(): jnp.einsum('kym,yj->kjm', moved, taps_matrix((y_total - 32) // 8), precis...  22.2 us
    unnamed x10, local copies, waits for them, and re-layouts  18.6 us
  transfers between devices with their start and end apart: 9, of which 8 were waited for; matrix products, arithmetic and copies ran while one was open for 5% of the time, Pallas kernels for 0%

profile of v1, /device:TPU:16, one launch (start us, length us, event | category | flops | bytes accessed | tf_op | source)
XLA Modules:
  0.0 670.2 jit_solution(6802573292930562529)
XLA Ops:
  1.3 11.3 %multiply_dynamic-update-slice_fusion.5 = f32[6,72,20,2048]{3,1,2,0:T(8,128)} fusion(f32[3,72,20,2048]{3,1,2,0:T(8,128)} %param.1), kind=kLoop, calls=%fused_computation.24 | loop fusion | flops 2949119 | bytes 23592960
  12.5 13.6 %multiply_dynamic-update-slice_fusion.4 = f32[6,72,20,2048]{3,1,2,0:T(8,128)} fusion(f32[6,72,20,2048]{3,1,2,0:T(8,128)} %multiply_dynamic-update-slice_fusion.5, f32[3,72,20,2048]{3,1,2,0:T(8,128)} %param.1), kind=kLoop, calls=%fused_computation.23 | loop fusion | flops 2949120 | bytes 35389440
  26.1 13.6 %multiply_dynamic-update-slice_fusion.3 = f32[6,72,20,2048]{3,1,2,0:T(8,128)} fusion(f32[6,72,20,2048]{3,1,2,0:T(8,128)} %multiply_dynamic-update-slice_fusion.4, f32[3,72,20,2048]{3,1,2,0:T(8,128)} %param.1), kind=kLoop, calls=%fused_computation.22 | loop fusion | flops 2949120 | bytes 35389440
  39.8 11.2 %multiply_dynamic-update-slice_fusion.2 = f32[6,72,20,2048]{3,1,2,0:T(8,128)} fusion(f32[6,72,20,2048]{3,1,2,0:T(8,128)} %multiply_dynamic-update-slice_fusion.3, f32[3,72,20,2048]{3,1,2,0:T(8,128)} %param.1), kind=kLoop, calls=%fused_computation.21 | loop fusion | flops 2949120 | bytes 23592960
  51.0 13.6 %multiply_dynamic-update-slice_fusion.1 = f32[6,72,20,2048]{3,1,2,0:T(8,128)} fusion(f32[6,72,20,2048]{3,1,2,0:T(8,128)} %multiply_dynamic-update-slice_fusion.2, f32[3,72,20,2048]{3,1,2,0:T(8,128)} %param.1), kind=kLoop, calls=%fused_computation.20 | loop fusion | flops 2949120 | bytes 35389440
  64.5 11.1 %multiply_dynamic-update-slice_fusion = f32[6,72,20,2048]{3,1,2,0:T(8,128)} fusion(f32[6,72,20,2048]{3,1,2,0:T(8,128)} %multiply_dynamic-update-slice_fusion.1, f32[3,72,20,2048]{3,1,2,0:T(8,128)} %param.1), kind=kLoop, calls=%fused_computation.19 | loop fusion | flops 2949120 | bytes 23592960 | tf_op jit(solution)/shard_map/stack | solution.py:86
  75.6 38.1 %convolution_bitcast_fusion.1 = f32[256,20,3,72]{0,3,1,2:T(8,128)} fusion(f32[3,72,20,2048]{3,1,2,0:T(8,128)} %param.1, f32[]{:T(128)} %fusion.104, s32[256]{0:T(256)S(1)} %iota_multiply_fusion), kind=kOutput, calls=%fused_computation.30 | convolution fusion | flops 27190624256 | bytes 39814148 | tf_op jit(solution)/shard_map/fzyn,nk->kyfz/dot_general | solution.py:61
  113.7 67.7 %convolution_bitcast_fusion = f32[256,20,6,72]{0,3,1,2:T(8,128)} fusion(f32[6,72,20,2048]{3,1,2,0:T(8,128)} %multiply_dynamic-update-slice_fusion, f32[]{:T(128)} %fusion.104, s32[256]{0:T(256)S(1)} %iota_multiply_fusion), kind=kOutput, calls=%fused_computation.25 | convolution fusion | flops 54369714176 | bytes 79627264 | tf_op jit(solution)/shard_map/fzyn,nk->kyfz/dot_general | solution.py:61
  181.4 14.5 %copy.17 = f32[256,20,6,72]{3,2,0,1:T(8,128)} copy(f32[256,20,6,72]{0,3,1,2:T(8,128)} %convolution_bitcast_fusion) | data formatting | bytes 17694720 | tf_op jit(solution)/shard_map/fzyn,nk->kyfz/transpose | solution.py:61
  196.0 17.9 %concatenate.9 = f32[8,32,20,432]{3,1,0,2:T(8,128)} reshape(f32[256,20,6,72]{3,2,0,1:T(8,128)} %copy.17) | data formatting | bytes 17694720 | tf_op jit(solution)/shard_map/concatenate | solution.py:91
  213.9 10.0 %copy.16 = f32[256,20,3,72]{3,2,0,1:T(4,128)} copy(f32[256,20,3,72]{0,3,1,2:T(8,128)} %convolution_bitcast_fusion.1) | data formatting | bytes 8847360 | tf_op jit(solution)/shard_map/fzyn,nk->kyfz/transpose | solution.py:61
  223.8 12.1 %concatenate.8 = f32[8,32,20,216]{3,1,0,2:T(8,128)} reshape(f32[256,20,3,72]{3,2,0,1:T(4,128)} %copy.16) | data formatting | bytes 8847360 | tf_op jit(solution)/shard_map/concatenate | solution.py:91
  236.0 8.3 %fusion.11 = (f32[32,20,648]{2,0,1:T(8,128)S(1)}, f32[32,20,648]{2,0,1:T(8,128)}, f32[32,20,648]{2,0,1:T(8,128)}, f32[32,20,648]{2,0,1:T(8,128)}, f32[32,20,648]{2,0,1:T(8,128)}, /*index=5*/f32[32,20,648]{2,0,1:T(8,128)}) fusion(s32[]{:T(128)S(6)} %select_n.76, f32[8,32,20,432]{3,1,0,2:T(8,128)} %concatenate.9, f32[8,32,20,216]{3,1,0,2:T(8,128)} %concatenate.8, ...), kind=kLoop, calls=%fused_computation.41 | loop fusion | flops 2488320 | bytes 23224344 | tf_op jit(solution)/shard_map/squeeze | solution.py:27
  247.8 3.8 collective-permute-start.4
  251.7 3.4 fusion.14
  256.9 32.5 %collective-permute-done = f32[32,20,648]{2,0,1:T(8,128)} collective-permute-done((f32[32,20,648]{2,0,1:T(8,128)}, f32[32,20,648]{2,0,1:T(8,128)}, u32[]{:S(2)}, u32[]{:S(2)}) %collective-permute-start) | collective-permute-done | bytes 1658912 | tf_op jit(solution)/shard_map/ppermute | solution.py:28
  289.9 82.8 %collective-permute-done.1 = f32[32,20,648]{2,0,1:T(8,128)} collective-permute-done((f32[32,20,648]{2,0,1:T(8,128)}, f32[32,20,648]{2,0,1:T(8,128)}, u32[]{:S(2)}, u32[]{:S(2)}) %collective-permute-start.1) | collective-permute-done | bytes 1658912 | tf_op jit(solution)/shard_map/ppermute | solution.py:28
  375.7 3.0 bitcast_dynamic-update-slice_fusion.5
  378.8 34.6 %collective-permute-done.2 = f32[32,20,648]{2,0,1:T(8,128)} collective-permute-done((f32[32,20,648]{2,0,1:T(8,128)}, f32[32,20,648]{2,0,1:T(8,128)}, u32[]{:S(2)}, u32[]{:S(2)}) %collective-permute-start.2) | collective-permute-done | bytes 1658912 | tf_op jit(solution)/shard_map/ppermute | solution.py:28
  413.4 3.0 bitcast_dynamic-update-slice_fusion.4
  416.4 3.1 bitcast_dynamic-update-slice_fusion.3
  419.5 82.5 %collective-permute-done.4 = f32[32,20,648]{2,0,1:T(8,128)} collective-permute-done((f32[32,20,648]{2,0,1:T(8,128)}, f32[32,20,648]{2,0,1:T(8,128)}, u32[]{:S(2)}, u32[]{:S(2)}) %collective-permute-start.4) | collective-permute-done | bytes 1658912 | tf_op jit(solution)/shard_map/ppermute | solution.py:28
  505.1 42.5 %collective-permute-done.5 = f32[32,20,648]{2,0,1:T(8,128)S(1)} collective-permute-done((f32[32,20,648]{2,0,1:T(8,128)S(1)}, f32[32,20,648]{2,0,1:T(8,128)S(1)}, u32[]{:S(2)}, u32[]{:S(2)}) %collective-permute-start.5) | collective-permute-done | bytes 1658912 | tf_op jit(solution)/shard_map/ppermute | solution.py:28
  549.1 39.5 %collective-permute-done.6 = f32[32,20,648]{2,0,1:T(8,128)S(1)} collective-permute-done((f32[32,20,648]{2,0,1:T(8,128)S(1)}, f32[32,20,648]{2,0,1:T(8,128)S(1)}, u32[]{:S(2)}, u32[]{:S(2)}) %collective-permute-start.6) | collective-permute-done | bytes 1658912 | tf_op jit(solution)/shard_map/ppermute | solution.py:28
  590.0 13.1 %gather_fusion = f32[8,32,20,648]{3,1,2,0:T(8,128)} fusion(f32[8,32,20,648]{3,1,2,0:T(8,128)} %bitcast_dynamic-update-slice_fusion, s32[1024]{0:T(1024)S(1)} %pad_clamp_fusion), kind=kCustom, calls=%fused_computation | custom fusion | bytes 26542112 | tf_op jit(solution)/shard_map/gather | solution.py:29
  603.2 22.2 %fusion.31 = f32[32,16,648]{2,1,0:T(8,128)S(1)} fusion(f32[32,160,648]{2,0,1:T(8,128)} %bitcast.108, f32[]{:T(128)} %fusion.104, f32[16]{0:T(128)S(1)} %convert_multiply_fusion, f32[160]{0:T(256)S(1)} %iota_convert_fusion), kind=kOutput, calls=%fused_computation.66 | convolution fusion | flops 637032960 | bytes 14598852 | tf_op jit(solution)/shard_map/kym,yj->kjm/dot_general | solution.py:67
  625.4 3.4 reshape.98
  632.1 4.4 all-to-all-start
  641.0 4.4 all-to-all-done
  645.4 3.5 all-to-all-start.1
  653.9 9.4 %all-to-all-done.1 = f32[32,16,432]{2,0,1:T(8,128)S(1)} async-done(((f32[32,16,432]{2,0,1:T(8,128)}), f32[32,16,432]{2,0,1:T(8,128)S(1)}, u32[]{:S(2)}, u32[]{:S(2)}) %all-to-all-start.1) | async-done | bytes 884768 | tf_op jit(solution)/shard_map/all_to_all | solution.py:98
  664.1 4.5 fusion.34
  (41 shorter events, 30.0 us)
Async XLA Ops:
  244.2 45.2 %collective-permute-start = (f32[32,20,648]{2,0,1:T(8,128)}, f32[32,20,648]{2,0,1:T(8,128)}, u32[]{:S(2)}, u32[]{:S(2)}) collective-permute-start(f32[32,20,648]{2,0,1:T(8,128)} %get-tuple-element.9), channel_id=1, source_target_pairs={{0,4},{4,0},{8,12},{12,8},{16,20},{20,16},{24,28},{28,24},{1,5},{5... | collective-permute-start | bytes 4976648 | tf_op jit(solution)/shard_map/ppermute | solution.py:28
  245.8 126.9 %collective-permute-start.1 = (f32[32,20,648]{2,0,1:T(8,128)}, f32[32,20,648]{2,0,1:T(8,128)}, u32[]{:S(2)}, u32[]{:S(2)}) collective-permute-start(f32[32,20,648]{2,0,1:T(8,128)} %get-tuple-element.10), channel_id=1, source_target_pairs={{0,8},{4,12},{8,0},{12,4},{16,24},{20,28},{24,16},{28,20},{1,9},{5... | collective-permute-start | bytes 4976648 | tf_op jit(solution)/shard_map/ppermute | solution.py:28
  247.4 166.0 %collective-permute-start.2 = (f32[32,20,648]{2,0,1:T(8,128)}, f32[32,20,648]{2,0,1:T(8,128)}, u32[]{:S(2)}, u32[]{:S(2)}) collective-permute-start(f32[32,20,648]{2,0,1:T(8,128)} %get-tuple-element.11), channel_id=1, source_target_pairs={{0,12},{4,8},{8,4},{12,0},{16,28},{20,24},{24,20},{28,16},{1,13},{... | collective-permute-start | bytes 4976648 | tf_op jit(solution)/shard_map/ppermute | solution.py:28
  247.8 168.6 %collective-permute-start.3 = (f32[32,20,648]{2,0,1:T(8,128)}, f32[32,20,648]{2,0,1:T(8,128)}, u32[]{:S(2)}, u32[]{:S(2)}) collective-permute-start(f32[32,20,648]{2,0,1:T(8,128)} %get-tuple-element.12), channel_id=1, source_target_pairs={{0,16},{4,20},{8,24},{12,28},{16,0},{20,4},{24,8},{28,12},{1,17},{... | collective-permute-start | bytes 4976648 | tf_op jit(solution)/shard_map/ppermute | solution.py:28
  247.8 254.3 %collective-permute-start.4 = (f32[32,20,648]{2,0,1:T(8,128)}, f32[32,20,648]{2,0,1:T(8,128)}, u32[]{:S(2)}, u32[]{:S(2)}) collective-permute-start(f32[32,20,648]{2,0,1:T(8,128)} %get-tuple-element.13), channel_id=1, source_target_pairs={{0,20},{4,16},{8,28},{12,24},{16,4},{20,0},{24,12},{28,8},{1,21},{... | collective-permute-start | bytes 4976648 | tf_op jit(solution)/shard_map/ppermute | solution.py:28
  251.7 3.5 copy-start
  289.5 258.1 %collective-permute-start.5 = (f32[32,20,648]{2,0,1:T(8,128)S(1)}, f32[32,20,648]{2,0,1:T(8,128)S(1)}, u32[]{:S(2)}, u32[]{:S(2)}) collective-permute-start(f32[32,20,648]{2,0,1:T(8,128)S(1)} %fusion.26), channel_id=1, source_target_pairs={{0,24},{4,28},{8,16},{12,20},{16,8},{20,12},{24,0},{28,4},{1,25},{... | collective-permute-start | bytes 4976648 | tf_op jit(solution)/shard_map/ppermute | solution.py:28
  372.7 215.9 %collective-permute-start.6 = (f32[32,20,648]{2,0,1:T(8,128)S(1)}, f32[32,20,648]{2,0,1:T(8,128)S(1)}, u32[]{:S(2)}, u32[]{:S(2)}) collective-permute-start(f32[32,20,648]{2,0,1:T(8,128)S(1)} %get-tuple-element.8), channel_id=1, source_target_pairs={{0,28},{4,24},{8,20},{12,16},{16,12},{20,8},{24,4},{28,0},{1,29},{... | collective-permute-start | bytes 4976648 | tf_op jit(solution)/shard_map/ppermute | solution.py:28
  632.1 13.3 %all-to-all-start = ((f32[32,16,216]{2,0,1:T(8,128)}), f32[32,16,216]{2,0,1:T(8,128)}, u32[]{:S(2)}, u32[]{:S(2)}) async-start(f32[32,16,216]{2,0,1:T(8,128)} %copy.21), calls=%async_computation | async-start | bytes 1048576 | tf_op jit(solution)/shard_map/all_to_all | solution.py:97
  645.4 18.0 %all-to-all-start.1 = ((f32[32,16,432]{2,0,1:T(8,128)}), f32[32,16,432]{2,0,1:T(8,128)S(1)}, u32[]{:S(2)}, u32[]{:S(2)}) async-start(f32[32,16,432]{2,0,1:T(8,128)} %copy.24), calls=%async_computation.1 | async-start | bytes 2097152 | tf_op jit(solution)/shard_map/all_to_all | solution.py:98
